TPU v7x, 768 devices: a whole 4x8x12 slice. The times are simulated.
768 devices in a mesh: space: 64 (over x, y, core), mp: 12 (over z).
Axes of the slice: x: 4, y: 8, z: 12, core: 2. Of those that a mesh axis runs over, the one named last changes fastest.
Arguments:
- tokens: bfloat16 [98304, 1024], P('space')
- norm_gain: float32 [1024], replicated, may hold values from 0.5 to 1.5
- w_qkv: bfloat16 [1024, 12, 192], P(None, 'mp')
- w_out: bfloat16 [768, 1024], replicated, may hold values from -0.75 to 0.75
- head_scale: float32 [12], P('mp'), may hold values from 8 to 400
- cycle_to_nested: int32 [98304], P('space'), may hold values from 0 to 98303, as said below
- neighbours: int32 [768, 9], P('space'), may hold values from -1 to 767, as said below
Outputs:
- mixed: bfloat16 [98304, 1024], P(('space', 'mp'))
Inputs may be any that keep to these rules, and one draw needn't show every extreme that they name: `cycle_to_nested`: A permutation of the tokens; the cycle rows of each index of space hold exactly 24 of the nested places of each index of space, the block of 1536 places of that index. `neighbours`: slot 0 names the block itself; the other slots name distinct other blocks at most 6 places away in block order, counted around the end of the order; only slots 7 and 8 may be -1.
All inputs are finite; a program needn't handle non-finite values.
Results may differ from a plain program's by a relative error of at most 0.012.
The roundings to bfloat16 on the way count: a program that leaves them out, or rounds other values in their place, can miss the bound.
Values may be sent and summed in bfloat16 or wider, within the bound.
A program may use at most 32 MiB of HBM per device.

v0:
```python
import jax
import jax.numpy as jnp
from jax import lax
from jax.sharding import PartitionSpec as P

BLOCK = 128
REACH = 6


def extended_2(shard, sides, width):
    for axis, dim in sides:
        size, length = (lax.axis_size(axis), shard.shape[dim])
        up = [(i, (i + 1) % size) for i in range(size)]
        down = [(j, i) for i, j in up]
        last = lax.slice_in_dim(shard, length - width, length, axis=dim)
        leading = lax.slice_in_dim(shard, 0, width, axis=dim)
        before = lax.ppermute(last, axis, up)
        after = lax.ppermute(leading, axis, down)
        shard = jnp.concatenate([before, shard, after], axis=dim)
    return shard


def norm_rows(tokens, norm_gain):
    values = tokens.astype(jnp.float32)
    mean_square = jnp.mean(values * values, axis=1, keepdims=True)
    return (values * lax.rsqrt(mean_square + 1e-05) * norm_gain).astype(jnp.bfloat16)


def project_head(normed, weight_head, scale_value, head_dim):
    projected = jnp.dot(normed, weight_head, preferred_element_type=jnp.float32)
    query_rows = projected[:, :head_dim]
    key_raw = projected[:, head_dim : 2 * head_dim]
    values = projected[:, 2 * head_dim :]
    query_rows = query_rows * (
        scale_value * lax.rsqrt(jnp.sum(query_rows * query_rows, axis=1, keepdims=True) + 1e-06)
    )
    key_raw = key_raw * lax.rsqrt(jnp.sum(key_raw * key_raw, axis=1, keepdims=True) + 1e-06)
    return jnp.concatenate([query_rows, key_raw, values], axis=1).astype(jnp.bfloat16)


def attend_blocks(query_rows, kv_blocks, positions, present, head_dim):
    block_rows = query_rows.shape[1]
    gathered = kv_blocks[positions]
    batch_blocks = gathered.shape[0]
    gathered_key_rows = gathered[..., :head_dim].reshape(batch_blocks, -1, head_dim)
    gathered_value_rows = gathered[..., head_dim:].reshape(batch_blocks, -1, head_dim)
    score_matrix = jnp.einsum(
        "ltv,lpv->ltp", query_rows, gathered_key_rows, preferred_element_type=jnp.float32
    )
    key_mask = jnp.repeat(present, block_rows, axis=1)[:, None, :]
    score_matrix = jnp.where(key_mask, score_matrix, -1e30)
    row_max = jnp.max(score_matrix, axis=2, keepdims=True)
    exponent = jnp.exp(score_matrix - row_max)
    row_total = jnp.sum(exponent, axis=2, keepdims=True)
    attention_weight = exponent.astype(jnp.bfloat16)
    weighted_sum = jnp.einsum(
        "uct,uth->uch", attention_weight, gathered_value_rows, preferred_element_type=jnp.float32
    )
    return (weighted_sum / row_total).astype(jnp.bfloat16)


def per_device(tokens, norm_gain, w_qkv, w_out, head_scale, cycle_to_nested, neighbours):
    tok_dev, model_width = tokens.shape
    space_count = lax.axis_size("space")
    head_dim = w_qkv.shape[2] // 3
    weight_head = w_qkv.reshape(model_width, 3 * head_dim)
    normed = norm_rows(tokens, norm_gain)
    row_order = jnp.argsort(cycle_to_nested)
    group_rows = tok_dev // space_count
    send_slots = cycle_to_nested[row_order].reshape(space_count, group_rows)
    base_slot = lax.axis_index("space") * tok_dev
    packed = project_head(normed, weight_head, head_scale[0], head_dim)
    send_rows = packed[row_order].reshape(space_count, group_rows, 3 * head_dim)
    got_rows, got_slots = (
        lax.all_to_all(send_rows, "space", split_axis=0, concat_axis=0, tiled=True),
        lax.all_to_all(send_slots, "space", split_axis=0, concat_axis=0, tiled=True),
    )
    slot_local = got_slots.reshape(-1) - base_slot
    nested_ordering = (
        jnp.zeros_like(packed).at[slot_local].set(got_rows.reshape(tok_dev, 3 * head_dim))
    )
    query_rows = nested_ordering[:, :head_dim].reshape(-1, BLOCK, head_dim)
    key_vals = nested_ordering[:, head_dim:]
    blk_count = tok_dev // BLOCK
    padding_blocks = REACH
    extended = extended_2(key_vals, (("space", 0),), REACH * BLOCK)
    kv_blocks = extended.reshape(blk_count + 2 * padding_blocks, BLOCK, 2 * head_dim)
    cycle_blocks = blk_count * space_count
    half_cycle = cycle_blocks // 2
    relative = (
        jnp.mod(neighbours - lax.axis_index("space") * blk_count + half_cycle, cycle_blocks)
        - half_cycle
    )
    present = neighbours >= 0
    positions = jnp.where(present, relative + padding_blocks, 0)
    attn = attend_blocks(query_rows, kv_blocks, positions, present, head_dim).reshape(
        tok_dev, head_dim
    )
    head_rows = lax.all_to_all(attn, "mp", split_axis=0, concat_axis=1, tiled=True)
    return jnp.dot(head_rows, w_out, preferred_element_type=jnp.float32).astype(jnp.bfloat16)


def solution(mesh):
    placed = (
        P("space", None),
        P(),
        P(None, "mp", None),
        P(),
        P("mp"),
        P("space"),
        P("space", None),
    )
    return jax.shard_map(
        per_device, mesh=mesh, in_specs=placed, out_specs=P(("space", "mp"), None), check_vma=False
    )
```

profile of v0, /device:TPU:1, one launch (start us, length us, event | category | flops | bytes accessed | tf_op | source)
XLA Modules:
  0.0 129.3 jit_solution(15189734282467065345)
XLA Ops:
  0.0 5.9 %sort.17 = (s32[1536]{0:T(1024)}, s32[1536]{0:T(1024)S(1)}) sort(s32[1536]{0:T(1024)} %param.12, s32[1536]{0:T(1024)S(1)} %iota.4), dimensions={0}, to_apply=%region_0.0 | sort | flops 16896 | bytes 24576 | tf_op jit(solution)/shard_map/jit(argsort)/sort | solution.py:68
  5.9 0.0 copy-start.5
  5.9 8.4 %gather_fusion = s32[1536]{0:T(1024)S(1)} fusion(s32[1536]{0:T(1024)S(1)} %copy-done.1, s32[2048]{0:T(1024)S(1)} %pad_clamp_fusion), kind=kCustom, calls=%fused_computation | custom fusion | bytes 18432 | tf_op jit(solution)/shard_map/gather | solution.py:70
  14.3 0.7 all_to_all.21
  15.0 14.5 %all-to-all-start = ((s32[64,1,24]{2,1,0:T(1,128)}), s32[64,1,24]{2,1,0:T(1,128)S(1)}, u32[]{:S(2)}, u32[]{:S(2)}) async-start(s32[64,1,24]{2,1,0:T(1,128)} %bitcast), calls=%async_computation | async-start | bytes 65536 | tf_op jit(solution)/shard_map/all_to_all | solution.py:76
  29.6 2.6 %fusion = f32[1536]{0:T(1024)S(1)} fusion(bf16[1536,1024]{1,0:T(8,128)(2,1)} %param.7), kind=kLoop, calls=%fused_computation.8 | loop fusion | flops 4717056 | bytes 3151872 | tf_op jit(solution)/shard_map/reduce_sum | solution.py:25
  32.2 3.2 %fusion.10 = f32[1536,192]{0,1:T(8,128)S(1)} fusion(bf16[1536,1024]{1,0:T(8,128)(2,1)} %param.7, f32[1024]{0:T(1024)S(1)} %copy-done.6, f32[1536]{0:T(1024)S(1)} %add_rsqrt_fusion.1, bf16[1024,1,192]{0,2,1:T(8,128)(2,1)S(1)} %copy-done.5), kind=kOutput, calls=%fused_computation.17 | convolution fusion | flops 610271232 | bytes 4728832 | tf_op jit(solution)/shard_map/dot_general | solution.py:30
  35.3 0.1 multiply_reduce_fusion.1
  36.1 0.1 multiply_convert_fusion.1
  36.2 0.3 copy.20
  36.5 5.3 %gather_fusion.1 = bf16[1536,192]{1,0:T(8,128)(2,1)} fusion(bf16[1536,192]{1,0:T(8,128)(2,1)S(1)} %copy.20, s32[2048]{0:T(1024)S(1)} %pad_clamp_fusion), kind=kCustom, calls=%fused_computation.1 | custom fusion | bytes 1185792 | tf_op jit(solution)/shard_map/gather | solution.py:73
  41.9 10.4 %all-to-all-start.1 = ((bf16[64,24,192]{2,1,0:T(8,128)(2,1)}), bf16[64,24,192]{2,1,0:T(8,128)(2,1)S(1)}, u32[]{:S(2)}, u32[]{:S(2)}) async-start(bf16[64,24,192]{2,1,0:T(8,128)(2,1)} %bitcast.3), calls=%async_computation.1 | async-start | bytes 1572864 | tf_op jit(solution)/shard_map/all_to_all | solution.py:75
  52.3 0.1 subtract_reduce_fusion
  52.4 0.1 sub.33
  52.6 22.7 %all-to-all-done.1 = bf16[64,24,192]{2,1,0:T(8,128)(2,1)S(1)} async-done(((bf16[64,24,192]{2,1,0:T(8,128)(2,1)}), bf16[64,24,192]{2,1,0:T(8,128)(2,1)S(1)}, u32[]{:S(2)}, u32[]{:S(2)}) %all-to-all-start.1) | async-done | bytes 589856 | tf_op jit(solution)/shard_map/all_to_all | solution.py:75
  75.3 7.3 %scatter_custom_fusion = bf16[1536,192]{1,0:T(8,128)(2,1)S(1)} fusion(s32[1536]{0:T(1024)S(1)} %fusion.25, bf16[1536,192]{1,0:T(8,128)(2,1)S(1)} %bitcast.30, bf16[]{:T(256)} %constant.17.clone.1), kind=kCustom, calls=%fused_computation.31 | custom fusion | bytes 589826 | tf_op jit(solution)/shard_map/scatter | solution.py:80
  82.6 0.2 fusion.28
  82.8 3.2 %collective-permute-start = (bf16[768,128]{1,0:T(8,128)(2,1)S(1)}, bf16[768,128]{1,0:T(8,128)(2,1)S(1)}, u32[]{:S(2)}, u32[]{:S(2)}) collective-permute-start(bf16[768,128]{1,0:T(8,128)(2,1)S(1)} %get-tuple-element.13), channel_id=1, source_target_pairs={{0,12},{12,24},{24,36},{36,48},{48,60},{60,72},{72,84},{84,96},{96... | collective-permute-start | bytes 589832 | tf_op jit(solution)/shard_map/ppermute | solution.py:17
  86.0 2.1 %collective-permute-start.1 = (bf16[768,128]{1,0:T(8,128)(2,1)S(1)}, bf16[768,128]{1,0:T(8,128)(2,1)S(1)}, u32[]{:S(2)}, u32[]{:S(2)}) collective-permute-start(bf16[768,128]{1,0:T(8,128)(2,1)S(1)} %get-tuple-element.14), channel_id=1, source_target_pairs={{12,0},{24,12},{36,24},{48,36},{60,48},{72,60},{84,72},{96,84},{10... | collective-permute-start | bytes 589832 | tf_op jit(solution)/shard_map/ppermute | solution.py:18
  88.1 0.1 reshape.104
  88.2 0.1 broadcast_in_dim.36
  88.3 0.6 copy.29
  89.0 0.2 slice.50
  89.1 4.0 %collective-permute-done.1 = bf16[768,128]{1,0:T(8,128)(2,1)S(1)} collective-permute-done((bf16[768,128]{1,0:T(8,128)(2,1)S(1)}, bf16[768,128]{1,0:T(8,128)(2,1)S(1)}, u32[]{:S(2)}, u32[]{:S(2)}) %collective-permute-start.1) | collective-permute-done | bytes 196640 | tf_op jit(solution)/shard_map/ppermute | solution.py:18
  93.1 0.1 pad_maximum_fusion
  93.2 2.8 %gather_fusion.2 = bf16[108,128,128]{2,1,0:T(8,128)(2,1)} fusion(bf16[24,128,128]{2,1,0:T(8,128)(2,1)S(1)} %bitcast.26, s32[1024]{0:T(1024)S(1)} %pad_clamp_fusion.1), kind=kCustom, calls=%fused_computation.2 | custom fusion | bytes 7078320 | tf_op jit(solution)/shard_map/gather | solution.py:43
  96.0 4.5 %fusion.27 = (bf16[12,9,128,64]{3,2,1,0:T(8,128)(2,1)S(1)}, bf16[12,9,128,64]{3,2,1,0:T(8,128)(2,1)S(1)}) fusion(bf16[12,9,128,128]{3,2,1,0:T(8,128)(2,1)} %bitcast.25), kind=kLoop, calls=%fused_computation.49 | loop fusion | bytes 7077888 | tf_op jit(solution)/shard_map/slice | solution.py:45
  100.5 1.3 select_reduce_fusion
  101.8 1.7 %fusion.3 = f32[12,128]{1,0:T(8,128)S(1)} fusion(f32[12,128,1152]{2,1,0:T(8,128)S(1)} %get-tuple-element.16, f32[12,128]{1,0:T(8,128)S(1)} %get-tuple-element.15, pred[12,1152]{1,0:T(8,128)(4,1)S(1)} %bitcast.33), kind=kLoop, calls=%fused_computation.11 | loop fusion | flops 5306880 | bytes 7104000 | tf_op jit(solution)/shard_map/reduce_sum | solution.py:54
  103.5 2.0 %fusion.17 = bf16[12,128,64]{1,2,0:T(8,128)(2,1)S(1)} fusion(bf16[12,1152,64]{2,1,0:T(8,128)(2,1)S(1)} %bitcast.29, f32[12,128,1152]{2,1,0:T(8,128)S(1)} %get-tuple-element.16, f32[12,128]{1,0:T(8,128)S(1)} %get-tuple-element.15, pred[12,1152]{1,0:T(8,128)(4,1)S(1)} %bitcast.34, f32[12,128]{1,0:T(8,128)S(1)} %fusion.3), kind=kOutput, calls=%fused_computation.22 | convolution fusion | flops 231997440 | bytes 9070080 | tf_op jit(solution)/shard_map/uct,uth->uch/dot_general | solution.py:56
  105.5 22.7 %all_to_all.30 = bf16[12,128,64]{1,2,0:T(8,128)(2,1)S(1)} all-to-all(bf16[12,128,64]{1,2,0:T(8,128)(2,1)S(1)} %fusion.17), channel_id=1, replica_groups=mesh['space'=64,'mp'=12] {'mp'}, dimensions={0} | all-to-all | bytes 393216 | tf_op jit(solution)/shard_map/all_to_all | solution.py:99
  128.2 1.1 convolution_convert_fusion
  (29 shorter events, 0.2 us)
Async XLA Ops:
  0.0 128.2 %copy-start = (bf16[768,1024]{1,0:T(8,128)(2,1)S(1)}, bf16[768,1024]{1,0:T(8,128)(2,1)}, u32[]{:S(2)}) copy-start(bf16[768,1024]{1,0:T(8,128)(2,1)} %param.10) | copy-start | bytes 4718596
  0.0 5.9 %copy-start.1 = (s32[1536]{0:T(1024)S(1)}, s32[1536]{0:T(1024)}, u32[]{:S(2)}) copy-start(s32[1536]{0:T(1024)} %param.12) | copy-start | bytes 18436
  5.9 26.3 %copy-start.5 = (bf16[1024,1,192]{0,2,1:T(8,128)(2,1)S(1)}, bf16[1024,1,192]{0,2,1:T(8,128)(2,1)}, u32[]{:S(2)}) copy-start(bf16[1024,1,192]{0,2,1:T(8,128)(2,1)} %param.9) | copy-start | bytes 1179652
  5.9 26.3 %copy-start.6 = (f32[1024]{0:T(1024)S(1)}, f32[1024]{0:T(1024)}, u32[]{:S(2)}) copy-start(f32[1024]{0:T(1024)} %param.8) | copy-start | bytes 12292
  15.0 26.8 %all-to-all-start = ((s32[64,1,24]{2,1,0:T(1,128)}), s32[64,1,24]{2,1,0:T(1,128)S(1)}, u32[]{:S(2)}, u32[]{:S(2)}) async-start(s32[64,1,24]{2,1,0:T(1,128)} %bitcast), calls=%async_computation | async-start | bytes 65536 | tf_op jit(solution)/shard_map/all_to_all | solution.py:76
  36.5 15.8 %copy-start.4 = (s32[12,9]{1,0:T(8,128)S(1)}, s32[12,9]{1,0:T(8,128)}, u32[]{:S(2)}) copy-start(s32[12,9]{1,0:T(8,128)} %param.13) | copy-start | bytes 1300
  41.9 33.4 %all-to-all-start.1 = ((bf16[64,24,192]{2,1,0:T(8,128)(2,1)}), bf16[64,24,192]{2,1,0:T(8,128)(2,1)S(1)}, u32[]{:S(2)}, u32[]{:S(2)}) async-start(bf16[64,24,192]{2,1,0:T(8,128)(2,1)} %bitcast.3), calls=%async_computation.1 | async-start | bytes 1572864 | tf_op jit(solution)/shard_map/all_to_all | solution.py:75
  82.6 13.4 %copy-start.2 = (bf16[1536,192]{1,0:T(8,128)(2,1)}, bf16[1536,192]{1,0:T(8,128)(2,1)S(1)}, u32[]{:S(2)}) copy-start(bf16[1536,192]{1,0:T(8,128)(2,1)S(1)} %scatter_custom_fusion) | copy-start | bytes 1769476
  82.8 6.3 %collective-permute-start = (bf16[768,128]{1,0:T(8,128)(2,1)S(1)}, bf16[768,128]{1,0:T(8,128)(2,1)S(1)}, u32[]{:S(2)}, u32[]{:S(2)}) collective-permute-start(bf16[768,128]{1,0:T(8,128)(2,1)S(1)} %get-tuple-element.13), channel_id=1, source_target_pairs={{0,12},{12,24},{24,36},{36,48},{48,60},{60,72},{72,84},{84,96},{96... | collective-permute-start | bytes 589832 | tf_op jit(solution)/shard_map/ppermute | solution.py:17
  86.0 7.1 %collective-permute-start.1 = (bf16[768,128]{1,0:T(8,128)(2,1)S(1)}, bf16[768,128]{1,0:T(8,128)(2,1)S(1)}, u32[]{:S(2)}, u32[]{:S(2)}) collective-permute-start(bf16[768,128]{1,0:T(8,128)(2,1)S(1)} %get-tuple-element.14), channel_id=1, source_target_pairs={{12,0},{24,12},{36,24},{48,36},{60,48},{72,60},{84,72},{96,84},{10... | collective-permute-start | bytes 589832 | tf_op jit(solution)/shard_map/ppermute | solution.py:18
  96.0 4.5 %slice-start = ((bf16[1536,192]{1,0:T(8,128)(2,1)}), bf16[1536,64]{1,0:T(8,128)(2,1)S(1)}, s32[]{:S(2)}) async-start(bf16[1536,192]{1,0:T(8,128)(2,1)} %copy-done.2), calls=%async_computation.3 | async-start | bytes 786432 | tf_op jit(solution)/shard_map/slice | solution.py:82
  96.0 4.5 %copy-start.3 = (pred[2,8,9,128]{3,1,2,0:T(8,128)(4,1)S(1)}, pred[2,8,9,128]{3,1,2,0:T(8,128)(4,1)}, u32[]{:S(2)}) copy-start(pred[2,8,9,128]{3,1,2,0:T(8,128)(4,1)} %copy.29) | copy-start | bytes 55300
where the time goes:
time: 131 us; the launch traced here: 129 us
  local copies, waits for them, and re-layouts  30.6 us (23%)
  starting transfers between devices  30.3 us (23%)
  waiting for transfers between devices  26.7 us (20%)
  blocking collectives  22.7 us (17%)
  other arithmetic  10.5 us (8%)
  matrix products  7.54 us (6%)
    all_to_all x1, waiting for transfers between devices, per_device(): lax.all_to_all(send_rows, 'space', split_axis=0, concat_axis=0, tiled=True)  22.7 us
    all_to_all x1, blocking collectives, per_device(): lax.all_to_all(attn, 'mp', split_axis=0, concat_axis=1, tiled=True)  22.7 us
    all_to_all x1, starting transfers between devices, per_device(): lax.all_to_all(send_slots, 'space', split_axis=0, concat_axis=0, tiled=True)  14.5 us
    all_to_all x1, starting transfers between devices, per_device(): lax.all_to_all(send_rows, 'space', split_axis=0, concat_axis=0, tiled=True)  10.4 us
    gather x1, local copies, waits for them, and re-layouts, per_device(): send_slots = cycle_to_nested[row_order].reshape(space_count, group_rows)  8.39 us
    scatter x1, local copies, waits for them, and re-layouts, per_device(): jnp.zeros_like(packed).at[slot_local]  7.32 us
    sort x1, other arithmetic, per_device(): row_order = jnp.argsort(cycle_to_nested)  5.86 us
    gather x1, local copies, waits for them, and re-layouts, per_device(): send_rows = packed[row_order].reshape(space_count, group_rows, 3 * head_dim)  5.34 us
  transfers between devices with their start and end apart: 4, of which 2 were waited for; matrix products, arithmetic and copies ran while one was open for 10% of the time, Pallas kernels for 0%

commit v1 on v0

v1 whole, which is shorter than its diff:
```python
import functools
import jax
import jax.numpy as jnp
from jax import lax
from jax.experimental import pallas as pl
from jax.experimental.pallas import tpu as pltpu
from jax.sharding import PartitionSpec as P

BLOCK = 128
REACH = 6
MASKED = 2
F32 = jnp.float32
BF16 = jnp.bfloat16
MESH = pl.DeviceIdType.MESH
NT = (((1,), (1,)), ((), ()))


def far_first(size, step):
    half = step // 2
    return jnp.where(step % 2 == 1, size // 2 - 1 - half, size // 2 + half) if size > 1 else 0 * step


def split_space(size):
    across = 4 if size == 64 else size // 4
    return across, size // 2 // across


def kernel(
    dims, tok_hbm, gain_ref, w_ref, wout_hbm, scale_ref, cyc_ref, nb_ref, out_ref,
    tok, wout, packed, place, send, recv, acc, query, keyval, attn, heads,
    tok_sem, wout_sem, ssem, rsem, hsem, grem, asem, arem,
):
    space, mp, reach = dims
    nx, ny = split_space(space)
    rows_dev, width = tok_hbm.shape
    hd = w_ref.shape[1] // 3
    group = rows_dev // space
    blocks = rows_dev // BLOCK
    nblk = blocks * space
    neigh = nb_ref.shape[1]
    tile = min(256, rows_dev)
    tiles = rows_dev // tile
    batch = min(16, space)
    batches = space // batch

    me, head = lax.axis_index("space"), lax.axis_index("mp")
    core, my_y, my_x = me % 2, (me // 2) % ny, me // (2 * ny)

    def displaced(j, sign):
        dc = far_first(2, j % 2)
        dx = far_first(nx, (j // 2) % nx)
        dy = far_first(ny, j // (2 * nx))
        x = (my_x + sign * dx + nx) % nx
        y = (my_y + sign * dy + ny) % ny
        return (x * ny + y) * 2 + (core + dc) % 2

    def ring(t):
        return (head + far_first(mp, t)) % mp

    def token_copy(i):
        part = pl.ds(pl.multiple_of(i * tile, tile), tile)
        return pltpu.make_async_copy(tok_hbm.at[part], tok.at[part], tok_sem.at[i])

    def exchange(j):
        return pltpu.make_async_remote_copy(
            src_ref=send.at[j], dst_ref=recv.at[j], send_sem=ssem.at[j], recv_sem=rsem.at[j],
            device_id=(displaced(j, 1), head), device_id_type=MESH,
        )

    def halo(side):
        if side == 0:
            src, dst, to = keyval.at[pl.ds(reach, reach)], keyval.at[pl.ds(reach + blocks, reach)], me + space - 1
        else:
            src, dst, to = keyval.at[pl.ds(blocks, reach)], keyval.at[pl.ds(0, reach)], me + 1
        return pltpu.make_async_remote_copy(
            src_ref=src, dst_ref=dst, send_sem=hsem.at[side], recv_sem=grem.at[side],
            device_id=(to % space, head), device_id_type=MESH,
        )

    def output_copy(t):
        return pltpu.make_async_remote_copy(
            src_ref=attn.at[t], dst_ref=heads.at[head], send_sem=asem.at[t], recv_sem=arem.at[t],
            device_id=(me, ring(t)), device_id_type=MESH,
        )

    def each(start, stop, body):
        lax.fori_loop(start, stop, lambda i, carry: (body(i), carry)[1], 0)

    barrier = pltpu.get_barrier_semaphore()
    each(0, space - 1, lambda j: pl.semaphore_signal(barrier, inc=1, device_id=(displaced(j, 1), head), device_id_type=MESH))
    each(0, mp - 1, lambda t: pl.semaphore_signal(barrier, inc=1, device_id=(me, ring(t)), device_id_type=MESH))

    each(0, tiles, lambda i: token_copy(i).start())
    wout_copy = pltpu.make_async_copy(wout_hbm, wout, wout_sem)
    wout_copy.start()

    step_ids = lax.broadcasted_iota(jnp.int32, (space, tile), 0)
    targets = displaced(step_ids, 1)
    before = jnp.where(
        lax.broadcasted_iota(jnp.int32, (tile, tile), 0) < lax.broadcasted_iota(jnp.int32, (tile, tile), 1), 1.0, 0.0
    ).astype(BF16)
    offset = step_ids.astype(F32) * group
    for i in range(tiles):
        cyc = cyc_ref[:, i * tile : (i + 1) * tile].astype(F32)
        owner = jnp.floor((cyc + 0.5) * (1.0 / rows_dev)).astype(jnp.int32)
        chosen = jnp.where(targets == owner, 1.0, 0.0)
        ahead = jnp.dot(chosen.astype(BF16), before, preferred_element_type=F32) + offset
        place[:, i * tile : (i + 1) * tile] = jnp.sum(chosen * ahead, axis=0, keepdims=True)
        offset = offset + jnp.sum(chosen, axis=1, keepdims=True)

    weight = w_ref[...]
    weight = jnp.concatenate([weight[:, hd:], weight[:, :hd], jnp.zeros((width, 2 * BLOCK - 3 * hd), BF16)], axis=1)
    lane = lax.broadcasted_iota(jnp.int32, (tile, BLOCK), 1)
    gain = gain_ref[...]
    scale = scale_ref[0]

    def project(i):
        token_copy(i).wait()
        part = pl.ds(pl.multiple_of(i * tile, tile), tile)
        values = tok[part].astype(F32)
        mean_square = jnp.mean(values * values, axis=1, keepdims=True)
        normed = (values * lax.rsqrt(mean_square + 1e-05) * gain).astype(BF16)
        projected = jnp.dot(normed, weight, preferred_element_type=F32)
        kv, q = projected[:, :BLOCK], projected[:, BLOCK:]
        key_square = jnp.sum(jnp.where(lane < hd, kv * kv, 0.0), axis=1, keepdims=True)
        kv = kv * jnp.where(lane < hd, lax.rsqrt(key_square + 1e-06), 1.0)
        q = q * (scale * lax.rsqrt(jnp.sum(q * q, axis=1, keepdims=True) + 1e-06))
        cyc = cyc_ref[:, part].astype(F32)
        cyc = jnp.concatenate(
            [jnp.broadcast_to(cyc[:, r : r + BLOCK], (BLOCK, BLOCK)).T for r in range(0, tile, BLOCK)], axis=0
        )
        slot = cyc - rows_dev * jnp.floor((cyc + 0.5) * (1.0 / rows_dev))
        upper = jnp.floor(slot * (1.0 / 64))
        q = jnp.where(lane == hd, upper, jnp.where(lane == hd + 1, slot - 64 * upper, q))
        packed[part] = jnp.concatenate([kv, q], axis=1).astype(BF16)

    each(0, tiles, project)

    def batch_of(g):
        rows = batch * group
        index = (lax.broadcasted_iota(jnp.int32, (rows, rows_dev), 0) + g * rows).astype(F32)
        pick = jnp.where(index == place[...], 1.0, 0.0).astype(BF16)
        ordered = jnp.dot(pick, packed[...], preferred_element_type=F32)
        parts = [ordered[:, :BLOCK].reshape(batch, group, BLOCK), ordered[:, BLOCK:].reshape(batch, group, BLOCK)]
        send[pl.ds(g * batch, batch)] = jnp.concatenate(parts, axis=1).astype(BF16)

    for g in range(batches):
        batch_of(g)
        if g == 0:
            pl.semaphore_wait(barrier, space - 1 + mp - 1)
        each(g * batch, min((g + 1) * batch, space - 1), lambda j: exchange(j).start())
    recv[space - 1] = send[space - 1]

    rows = batch * group
    lane8 = lax.broadcasted_iota(jnp.int32, (8, BLOCK), 1)
    decode = jnp.where(lane8 == hd, 64.0, jnp.where(lane8 == hd + 1, 1.0, 0.0)).astype(BF16)
    per_tile = tile // BLOCK
    for g in range(batches):
        each(g * batch, min((g + 1) * batch, space - 1), lambda j: exchange(j).wait_recv())
        got = recv[pl.ds(g * batch, batch)].astype(F32)
        kv = got[:, :group].reshape(rows, BLOCK)
        q = got[:, group:].reshape(rows, BLOCK)
        slot = lax.dot_general(decode, q.astype(BF16), NT, preferred_element_type=F32)[:1]
        got = jnp.concatenate([kv, q], axis=1).astype(BF16)
        for i in range(tiles):
            part = pl.ds(i * tile, tile)
            index = (lax.broadcasted_iota(jnp.int32, (tile, rows), 0) + i * tile).astype(F32)
            pick = jnp.where(index == slot, 1.0, 0.0).astype(BF16)
            found = jnp.dot(pick, got, preferred_element_type=F32)
            if g > 0:
                found = acc[part] + found
            if g < batches - 1:
                acc[part] = found
            else:
                kv = found[:, :BLOCK].astype(BF16)
                q = jnp.where(lane < hd, found[:, BLOCK:], 0.0).astype(BF16)
                keyval[pl.ds(reach + i * per_tile, per_tile)] = kv.reshape(per_tile, BLOCK, BLOCK)
                query[pl.ds(i * per_tile, per_tile)] = q.reshape(per_tile, BLOCK, BLOCK)
                if (i + 1) * per_tile >= reach > i * per_tile:
                    halo(0).start()
    halo(1).start()
    halo(0).wait_recv()
    halo(1).wait_recv()

    lane_half = lax.broadcasted_iota(jnp.int32, (BLOCK // 2, BLOCK), 1)

    def attend(b):
        kvs, absent = [], []
        for s in range(neigh):
            nb = nb_ref[b, s]
            at = (nb - me * blocks + nblk // 2 + nblk) % nblk - nblk // 2 + reach
            kvs.append(keyval[jnp.clip(jnp.where(nb >= 0, at, 0), 0, blocks + 2 * reach - 1)])
            absent.append(jnp.where(nb >= 0, 0.0, -1e30))
        kvs = jnp.concatenate(kvs, axis=0)
        scores = lax.dot_general(query[b], kvs, NT, preferred_element_type=F32)
        cut = (neigh - MASKED) * BLOCK
        tail = [scores[:, s * BLOCK : (s + 1) * BLOCK] + absent[s] for s in range(neigh - MASKED, neigh)]
        scores = jnp.concatenate([scores[:, :cut], *tail], axis=1)
        weights = jnp.exp(scores - jnp.max(scores, axis=1, keepdims=True))
        total = jnp.sum(weights, axis=1, keepdims=True)
        mixed = jnp.dot(weights.astype(BF16), kvs, preferred_element_type=F32) / total
        half = BLOCK // 2
        return jnp.where(lane_half < hd, pltpu.roll(mixed[:half], hd, 1), mixed[half:]).astype(BF16)

    def attend_send(t):
        attn[t] = attend(ring(t))
        output_copy(t).start()

    each(0, mp - 1, attend_send)
    heads[head] = attend(head)
    wout_copy.wait()
    each(0, mp - 1, lambda t: output_copy(t).wait_recv())

    halves = [], []
    for h in range(0, mp, 2):
        low, high = heads[h].astype(F32), heads[h + 1].astype(F32)
        halves[0].append(jnp.where(lane_half < hd, low, pltpu.roll(high, hd, 1)))
        halves[1].append(jnp.where(lane_half < hd, pltpu.roll(low, hd, 1), high))
    rows_in = jnp.concatenate([jnp.concatenate(part, axis=1) for part in halves], axis=0).astype(BF16)
    out_ref[...] = jnp.dot(rows_in, wout[...], preferred_element_type=F32).astype(BF16)

    each(0, space - 1, lambda j: exchange(j).wait_send())
    halo(0).wait_send()
    halo(1).wait_send()
    each(0, mp - 1, lambda t: output_copy(t).wait_send())


def per_device(reach, tokens, norm_gain, w_qkv, w_out, head_scale, cycle_to_nested, neighbours):
    space, mp = lax.axis_size("space"), lax.axis_size("mp")
    rows, width = tokens.shape
    wide = w_out.shape[1]
    group, blocks = rows // space, rows // BLOCK
    tiles = rows // min(256, rows)
    vmem, smem, anywhere = (pl.BlockSpec(memory_space=m) for m in (pltpu.VMEM, pltpu.SMEM, pl.ANY))
    dma = pltpu.SemaphoreType.DMA
    return pl.pallas_call(
        functools.partial(kernel, (space, mp, reach)),
        out_shape=jax.ShapeDtypeStruct((rows // mp, wide), BF16),
        in_specs=[anywhere, vmem, vmem, anywhere, smem, vmem, smem],
        out_specs=vmem,
        scratch_shapes=[
            pltpu.VMEM(tokens.shape, BF16),
            pltpu.VMEM(w_out.shape, BF16),
            pltpu.VMEM((rows, 2 * BLOCK), BF16),
            pltpu.VMEM((1, rows), F32),
            pltpu.VMEM((space, 2 * group, BLOCK), BF16),
            pltpu.VMEM((space, 2 * group, BLOCK), BF16),
            pltpu.VMEM((rows, 2 * BLOCK), F32),
            pltpu.VMEM((blocks, BLOCK, BLOCK), BF16),
            pltpu.VMEM((blocks + 2 * reach, BLOCK, BLOCK), BF16),
            pltpu.VMEM((mp, BLOCK // 2, BLOCK), BF16),
            pltpu.VMEM((mp, BLOCK // 2, BLOCK), BF16),
            dma((tiles,)), dma, dma((space,)), dma((space,)), dma((2,)), dma((2,)), dma((mp,)), dma((mp,)),
        ],
        compiler_params=pltpu.CompilerParams(collective_id=0, has_side_effects=True, vmem_limit_bytes=56 * 2**20),
    )(
        tokens, norm_gain.reshape(1, width), w_qkv.reshape(width, -1), w_out, head_scale,
        cycle_to_nested.reshape(1, rows), neighbours,
    )


def solution(mesh, reach=REACH):
    placed = (P("space", None), P(), P(None, "mp", None), P(), P("mp"), P("space"), P("space", None))
    return jax.shard_map(
        functools.partial(per_device, reach), mesh=mesh, in_specs=placed, out_specs=P(("space", "mp"), None), check_vma=False
    )
```

time: 131 us -> 69 us (0.53); the launches traced: 129 us -> 68.7 us
  Pallas kernels: 0 us -> 63 us
  starting transfers between devices: 30.3 us -> 0 us
  waiting for transfers between devices: 26.7 us -> 0 us
  local copies, waits for them, and re-layouts: 30.6 us -> 4.95 us
  blocking collectives: 22.7 us -> 0 us
  other arithmetic: 10.5 us -> 0 us
  matrix products: 7.54 us -> 0 us
    pallas_call x0 -> x1, Pallas kernels: none -> 63 us  [per_device(): pl.pallas_call(functools.partial(kernel, (space, mp, reach)), out_shape=j...]
    all_to_all x2 -> x0, starting transfers between devices: 25 us -> none  [the longest x1 14.5 us: per_device(): lax.all_to_all(send_slots, 'space', split_axis=0, concat_axis=0, tiled=True)]
    all_to_all x2 -> x0, waiting for transfers between devices: 22.7 us -> none  [the longest x1 22.7 us: per_device(): lax.all_to_all(send_rows, 'space', split_axis=0, concat_axis=0, tiled=True)]
    all_to_all x1 -> x0, blocking collectives: 22.7 us -> none  [per_device(): lax.all_to_all(attn, 'mp', split_axis=0, concat_axis=1, tiled=True)]
    gather x3 -> x0, local copies, waits for them, and re-layouts: 16.6 us -> none  [the longest x1 8.39 us: per_device(): send_slots = cycle_to_nested[row_order].reshape(space_count, group_rows)]
    dot_general x4 -> x0, matrix products: 7.54 us -> none  [the longest x1 3.16 us: project_head(): projected = jnp.dot(normed, weight_head, preferred_element_type=jnp.float32)]
    scatter x1 -> x0, local copies, waits for them, and re-layouts: 7.32 us -> none  [per_device(): jnp.zeros_like(packed).at[slot_local]]
    sort x1 -> x0, other arithmetic: 5.86 us -> none  [per_device(): row_order = jnp.argsort(cycle_to_nested)]
  transfers between devices with their start and end apart: 4 -> 0, of which waited for: 2 -> 0; matrix products, arithmetic and copies ran while one was open for 10% -> 0% of each run, Pallas kernels for 0% -> 0%
where the time goes in v1:
time: 69 us; the launch traced here: 68.7 us
  Pallas kernels  63 us (91%)
  local copies, waits for them, and re-layouts  4.95 us (7%)
    pallas_call x1, Pallas kernels, per_device(): pl.pallas_call(functools.partial(kernel, (space, mp, reach)), out_shape=j...  63 us
    unnamed x2, local copies, waits for them, and re-layouts  3.66 us

profile of v1, /device:TPU:1, one launch (start us, length us, event | category | flops | bytes accessed | tf_op | source)
XLA Modules:
  0.0 68.7 jit_solution(933051789774928257)
XLA Ops:
  0.7 1.3 %reshape.11.cyc_ref = s32[1,1536]{1,0:T(1,128)} reshape(s32[1536]{0:T(1024)} %param.12) | data formatting | bytes 12288 | tf_op jit(solution)/shard_map/reshape | solution.py:258
  1.9 2.0 %copy.8 = bf16[1024,1,192]{2,0,1:T(8,128)(2,1)} copy(bf16[1024,1,192]{0,2,1:T(8,128)(2,1)} %param.9) | data formatting | bytes 786432 | tf_op args[2]
  3.9 63.0 %shard_map.73 = bf16[128,1024]{1,0:T(8,128)(2,1)} custom-call(bf16[1536,1024]{1,0:T(8,128)(2,1)} %tok_hbm.1, f32[1,1024]{1,0:T(1,128)} %bitcast.3, bf16[1024,192]{1,0:T(8,128)(2,1)} %bitcast.2, bf16[768,1024]{1,0:T(8,128)(2,1)} %wout_hbm.1, f32[1]{0:T(128)S(6)} %copy.10.scale_ref, s32[1,1536]{1,0:T(1,128)} %reshape.11.cyc_ref, s32[12,9]{1,0:T(8,128)} %nb_ref.1), custom_call_target="tpu_custom_call" | custom-call | tf_op jit(solution)/shard_map/pallas_call | solution.py:236
  67.0 1.7 %copy.11 = bf16[128,1024]{1,0:T(8,128)(2,1)} copy(bf16[128,1024]{1,0:T(8,128)(2,1)} %shard_map.73) | data formatting | bytes 524288

commit v2 on v1

--- a/solution.py
+++ b/solution.py
@@ -17,6 +17,8 @@
 
 def far_first(size, step):
     half = step // 2
+    if size % 2:
+        return (step + 1) % size
     return jnp.where(step % 2 == 1, size // 2 - 1 - half, size // 2 + half) if size > 1 else 0 * step
 
 
@@ -27,32 +29,31 @@
 
 def kernel(
     dims, tok_hbm, gain_ref, w_ref, wout_hbm, scale_ref, cyc_ref, nb_ref, out_ref,
-    tok, wout, packed, place, send, recv, acc, query, keyval, attn, heads,
-    tok_sem, wout_sem, ssem, rsem, hsem, grem, asem, arem,
+    tok, wout, packed, place, trade, send, recv, acc, query, keyval, attn, heads,
+    tok_sem, wout_sem, csem, drem, ssem, rsem, hsem, grem, asem, arem,
 ):
     space, mp, reach = dims
     nx, ny = split_space(space)
     rows_dev, width = tok_hbm.shape
-    hd = w_ref.shape[1] // 3
+    hd = w_ref.shape[0] // 3
     group = rows_dev // space
     blocks = rows_dev // BLOCK
     nblk = blocks * space
     neigh = nb_ref.shape[1]
     tile = min(256, rows_dev)
     tiles = rows_dev // tile
-    batch = min(16, space)
-    batches = space // batch
+    chips = space // 2
+    batch = max(1, chips // 4)
+    batches = chips // batch
+    third = group // 3
 
     me, head = lax.axis_index("space"), lax.axis_index("mp")
     core, my_y, my_x = me % 2, (me // 2) % ny, me // (2 * ny)
 
-    def displaced(j, sign):
-        dc = far_first(2, j % 2)
-        dx = far_first(nx, (j // 2) % nx)
-        dy = far_first(ny, j // (2 * nx))
-        x = (my_x + sign * dx + nx) % nx
-        y = (my_y + sign * dy + ny) % ny
-        return (x * ny + y) * 2 + (core + dc) % 2
+    def displaced(j):
+        x = (my_x + far_first(nx, j % nx)) % nx
+        y = (my_y + far_first(ny, j // nx)) % ny
+        return x * ny + y
 
     def ring(t):
         return (head + far_first(mp, t)) % mp
@@ -61,10 +62,16 @@
         part = pl.ds(pl.multiple_of(i * tile, tile), tile)
         return pltpu.make_async_copy(tok_hbm.at[part], tok.at[part], tok_sem.at[i])
 
+    def core_trade(g):
+        return pltpu.make_async_remote_copy(
+            src_ref=trade.at[g], dst_ref=send.at[pl.ds(g * batch, batch), core], send_sem=csem.at[g], recv_sem=drem.at[g],
+            device_id=(me + 1 - 2 * core, head), device_id_type=MESH,
+        )
+
     def exchange(j):
         return pltpu.make_async_remote_copy(
             src_ref=send.at[j], dst_ref=recv.at[j], send_sem=ssem.at[j], recv_sem=rsem.at[j],
-            device_id=(displaced(j, 1), head), device_id_type=MESH,
+            device_id=(displaced(j) * 2 + core, head), device_id_type=MESH,
         )
 
     def halo(side):
@@ -87,7 +94,9 @@
         lax.fori_loop(start, stop, lambda i, carry: (body(i), carry)[1], 0)
 
     barrier = pltpu.get_barrier_semaphore()
-    each(0, space - 1, lambda j: pl.semaphore_signal(barrier, inc=1, device_id=(displaced(j, 1), head), device_id_type=MESH))
+    each(0, chips - 1, lambda j: pl.semaphore_signal(barrier, inc=1, device_id=(displaced(j) * 2 + core, head), device_id_type=MESH))
+    pl.semaphore_signal(barrier, inc=1, device_id=((me + 1) % space, head), device_id_type=MESH)
+    pl.semaphore_signal(barrier, inc=1, device_id=((me + space - 1) % space, head), device_id_type=MESH)
     each(0, mp - 1, lambda t: pl.semaphore_signal(barrier, inc=1, device_id=(me, ring(t)), device_id_type=MESH))
 
     each(0, tiles, lambda i: token_copy(i).start())
@@ -95,13 +104,13 @@
     wout_copy.start()
 
     step_ids = lax.broadcasted_iota(jnp.int32, (space, tile), 0)
-    targets = displaced(step_ids, 1)
+    targets = displaced(step_ids // (2 * batch) * batch + step_ids % batch) * 2 + (core + 1 - step_ids // batch % 2) % 2
     before = jnp.where(
         lax.broadcasted_iota(jnp.int32, (tile, tile), 0) < lax.broadcasted_iota(jnp.int32, (tile, tile), 1), 1.0, 0.0
     ).astype(BF16)
     offset = step_ids.astype(F32) * group
     for i in range(tiles):
-        cyc = cyc_ref[:, i * tile : (i + 1) * tile].astype(F32)
+        cyc = cyc_ref[pl.ds(i * tile, tile)].reshape(1, tile).astype(F32)
         owner = jnp.floor((cyc + 0.5) * (1.0 / rows_dev)).astype(jnp.int32)
         chosen = jnp.where(targets == owner, 1.0, 0.0)
         ahead = jnp.dot(chosen.astype(BF16), before, preferred_element_type=F32) + offset
@@ -109,7 +118,7 @@
         offset = offset + jnp.sum(chosen, axis=1, keepdims=True)
 
     weight = w_ref[...]
-    weight = jnp.concatenate([weight[:, hd:], weight[:, :hd], jnp.zeros((width, 2 * BLOCK - 3 * hd), BF16)], axis=1)
+    weight = jnp.concatenate([weight[hd:], weight[:hd], jnp.zeros((2 * BLOCK - 3 * hd, width), BF16)], axis=0)
     lane = lax.broadcasted_iota(jnp.int32, (tile, BLOCK), 1)
     gain = gain_ref[...]
     scale = scale_ref[0]
@@ -120,12 +129,12 @@
         values = tok[part].astype(F32)
         mean_square = jnp.mean(values * values, axis=1, keepdims=True)
         normed = (values * lax.rsqrt(mean_square + 1e-05) * gain).astype(BF16)
-        projected = jnp.dot(normed, weight, preferred_element_type=F32)
+        projected = lax.dot_general(normed, weight, NT, preferred_element_type=F32)
         kv, q = projected[:, :BLOCK], projected[:, BLOCK:]
         key_square = jnp.sum(jnp.where(lane < hd, kv * kv, 0.0), axis=1, keepdims=True)
         kv = kv * jnp.where(lane < hd, lax.rsqrt(key_square + 1e-06), 1.0)
         q = q * (scale * lax.rsqrt(jnp.sum(q * q, axis=1, keepdims=True) + 1e-06))
-        cyc = cyc_ref[:, part].astype(F32)
+        cyc = cyc_ref[part].reshape(1, tile).astype(F32)
         cyc = jnp.concatenate(
             [jnp.broadcast_to(cyc[:, r : r + BLOCK], (BLOCK, BLOCK)).T for r in range(0, tile, BLOCK)], axis=0
         )
@@ -136,30 +145,56 @@
 
     each(0, tiles, project)
 
-    def batch_of(g):
-        rows = batch * group
+    def spread(values):
+        return values.reshape(-1, group, BLOCK)
+
+    def message(kv, q):
+        first, second, last = q[:, :third], q[:, third : 2 * third], q[:, 2 * third :]
+        lanes = lax.broadcasted_iota(jnp.int32, first.shape, 2)
+        pairs = jnp.where(lanes < hd, first, pltpu.roll(second, hd, 2))
+        last = jnp.where((lanes == hd + 2) | (lanes == hd + 3), pltpu.roll(first, 2, 2), last)
+        last = jnp.where((lanes == hd + 4) | (lanes == hd + 5), pltpu.roll(second, 4, 2), last)
+        return jnp.concatenate([kv, pairs, last], axis=1).astype(BF16)
+
+    def from_message(got):
+        pairs, last = got[:, group : group + third], got[:, group + third :]
+        lanes = lax.broadcasted_iota(jnp.int32, pairs.shape, 2)
+        first = jnp.where(lanes < hd, pairs, pltpu.roll(last, BLOCK - 2, 2))
+        second = jnp.where(lanes < hd, pltpu.roll(pairs, hd, 2), pltpu.roll(last, BLOCK - 4, 2))
+        return got[:, :group], jnp.concatenate([first, second, last], axis=1)
+
+    rows = 2 * batch * group
+
+    def order_rows(g):
         index = (lax.broadcasted_iota(jnp.int32, (rows, rows_dev), 0) + g * rows).astype(F32)
         pick = jnp.where(index == place[...], 1.0, 0.0).astype(BF16)
         ordered = jnp.dot(pick, packed[...], preferred_element_type=F32)
-        parts = [ordered[:, :BLOCK].reshape(batch, group, BLOCK), ordered[:, BLOCK:].reshape(batch, group, BLOCK)]
-        send[pl.ds(g * batch, batch)] = jnp.concatenate(parts, axis=1).astype(BF16)
+        made = message(spread(ordered[:, :BLOCK]), spread(ordered[:, BLOCK:]))
+        trade[g] = made[:batch]
+        send[pl.ds(g * batch, batch), core] = made[batch:]
+
+    def send_batch(g):
+        core_trade(g).wait_recv()
+        each(g * batch, min((g + 1) * batch, chips - 1), lambda j: exchange(j).start())
 
     for g in range(batches):
-        batch_of(g)
+        order_rows(g)
         if g == 0:
-            pl.semaphore_wait(barrier, space - 1 + mp - 1)
-        each(g * batch, min((g + 1) * batch, space - 1), lambda j: exchange(j).start())
-    recv[space - 1] = send[space - 1]
-
-    rows = batch * group
+            pl.semaphore_wait(barrier, chips - 1 + 2 + mp - 1)
+        core_trade(g).start()
+        if g > 0:
+            send_batch(g - 1)
+    send_batch(batches - 1)
+    recv[chips - 1] = send[chips - 1]
+
     lane8 = lax.broadcasted_iota(jnp.int32, (8, BLOCK), 1)
     decode = jnp.where(lane8 == hd, 64.0, jnp.where(lane8 == hd + 1, 1.0, 0.0)).astype(BF16)
     per_tile = tile // BLOCK
     for g in range(batches):
-        each(g * batch, min((g + 1) * batch, space - 1), lambda j: exchange(j).wait_recv())
+        each(g * batch, min((g + 1) * batch, chips - 1), lambda j: exchange(j).wait_recv())
         got = recv[pl.ds(g * batch, batch)].astype(F32)
-        kv = got[:, :group].reshape(rows, BLOCK)
-        q = got[:, group:].reshape(rows, BLOCK)
+        kv, q = from_message(got.reshape(2 * batch, group + 2 * third, BLOCK))
+        kv, q = kv.reshape(rows, BLOCK), q.reshape(rows, BLOCK)
         slot = lax.dot_general(decode, q.astype(BF16), NT, preferred_element_type=F32)[:1]
         got = jnp.concatenate([kv, q], axis=1).astype(BF16)
         for i in range(tiles):
@@ -219,7 +254,8 @@
     rows_in = jnp.concatenate([jnp.concatenate(part, axis=1) for part in halves], axis=0).astype(BF16)
     out_ref[...] = jnp.dot(rows_in, wout[...], preferred_element_type=F32).astype(BF16)
 
-    each(0, space - 1, lambda j: exchange(j).wait_send())
+    each(0, batches, lambda g: core_trade(g).wait_send())
+    each(0, chips - 1, lambda j: exchange(j).wait_send())
     halo(0).wait_send()
     halo(1).wait_send()
     each(0, mp - 1, lambda t: output_copy(t).wait_send())
@@ -231,6 +267,9 @@
     wide = w_out.shape[1]
     group, blocks = rows // space, rows // BLOCK
     tiles = rows // min(256, rows)
+    chips = space // 2
+    batch = max(1, chips // 4)
+    batches, message = chips // batch, group + 2 * (group // 3)
     vmem, smem, anywhere = (pl.BlockSpec(memory_space=m) for m in (pltpu.VMEM, pltpu.SMEM, pl.ANY))
     dma = pltpu.SemaphoreType.DMA
     return pl.pallas_call(
@@ -243,19 +282,20 @@
             pltpu.VMEM(w_out.shape, BF16),
             pltpu.VMEM((rows, 2 * BLOCK), BF16),
             pltpu.VMEM((1, rows), F32),
-            pltpu.VMEM((space, 2 * group, BLOCK), BF16),
-            pltpu.VMEM((space, 2 * group, BLOCK), BF16),
+            pltpu.VMEM((batches, batch, message, BLOCK), BF16),
+            pltpu.VMEM((chips, 2, message, BLOCK), BF16),
+            pltpu.VMEM((chips, 2, message, BLOCK), BF16),
             pltpu.VMEM((rows, 2 * BLOCK), F32),
             pltpu.VMEM((blocks, BLOCK, BLOCK), BF16),
             pltpu.VMEM((blocks + 2 * reach, BLOCK, BLOCK), BF16),
             pltpu.VMEM((mp, BLOCK // 2, BLOCK), BF16),
             pltpu.VMEM((mp, BLOCK // 2, BLOCK), BF16),
-            dma((tiles,)), dma, dma((space,)), dma((space,)), dma((2,)), dma((2,)), dma((mp,)), dma((mp,)),
+            dma((tiles,)), dma, dma((batches,)), dma((batches,)), dma((chips,)), dma((chips,)), dma((2,)), dma((2,)), dma((mp,)), dma((mp,)),
         ],
         compiler_params=pltpu.CompilerParams(collective_id=0, has_side_effects=True, vmem_limit_bytes=56 * 2**20),
     )(
-        tokens, norm_gain.reshape(1, width), w_qkv.reshape(width, -1), w_out, head_scale,
-        cycle_to_nested.reshape(1, rows), neighbours,
+        tokens, norm_gain.reshape(1, width), w_qkv.transpose(1, 2, 0).reshape(-1, width), w_out, head_scale,
+        cycle_to_nested, neighbours,
     )
 
 

time: 69 us -> 61.4 us (0.89)
  Pallas kernels: 63 us -> 58.9 us
  local copies, waits for them, and re-layouts: 4.95 us -> 1.67 us
    pallas_call x1, Pallas kernels: 63 us -> 58.9 us  [per_device(): pl.pallas_call(functools.partial(kernel, (space, mp, reach)), out_shape=j...]
    unnamed x2 -> x1, local copies, waits for them, and re-layouts: 3.66 us -> 1.67 us
    reshape x1 -> x0, local copies, waits for them, and re-layouts: 1.29 us -> none  [per_device(): cycle_to_nested.reshape(1, rows)]
where the time goes in v2:
time: 61.4 us; the launch traced here: 61.3 us
  Pallas kernels  58.9 us (96%)
  local copies, waits for them, and re-layouts  1.67 us (3%)
  between operations  0.66 us (1%)
    pallas_call x1, Pallas kernels, per_device(): pl.pallas_call(functools.partial(kernel, (space, mp, reach)), out_shape=j...  58.9 us
    unnamed x1, local copies, waits for them, and re-layouts  1.67 us

profile of v2, /device:TPU:1, one launch (start us, length us, event | category | flops | bytes accessed | tf_op | source)
XLA Modules:
  0.0 61.3 jit_solution(9699749809091074747)
XLA Ops:
  0.7 58.9 %shard_map.73 = bf16[128,1024]{1,0:T(8,128)(2,1)} custom-call(bf16[1536,1024]{1,0:T(8,128)(2,1)} %tok_hbm.1, f32[1,1024]{1,0:T(1,128)} %bitcast.5, bf16[192,1024]{1,0:T(8,128)(2,1)} %bitcast.4, bf16[768,1024]{1,0:T(8,128)(2,1)} %wout_hbm.1, f32[1]{0:T(128)S(6)} %copy.9.scale_ref, s32[1536]{0:T(1024)} %cyc_ref.1, s32[12,9]{1,0:T(8,128)} %nb_ref.1), custom_call_target="tpu_custom_call" | custom-call | tf_op jit(solution)/shard_map/pallas_call | solution.py:275
  59.6 1.7 %copy.10 = bf16[128,1024]{1,0:T(8,128)(2,1)} copy(bf16[128,1024]{1,0:T(8,128)(2,1)} %shard_map.73) | data formatting | bytes 524288

commit v3 on v2

--- a/solution.py
+++ b/solution.py
@@ -15,11 +15,21 @@
 NT = (((1,), (1,)), ((), ()))
 
 
-def far_first(size, step):
-    half = step // 2
+def far_static(size, step):
     if size % 2:
         return (step + 1) % size
-    return jnp.where(step % 2 == 1, size // 2 - 1 - half, size // 2 + half) if size > 1 else 0 * step
+    return size // 2 - 1 - step // 2 if step % 2 else size // 2 + step // 2
+
+
+def chip_steps(nx, ny):
+    xs = [far_static(nx, i) if nx > 1 else 0 for i in range(nx)]
+    steps = [(dx, ny // 2) for dx in xs]
+    same = [(dx, 0) for dx in xs if dx]
+    for level in range(ny // 2 - 1, 0, -1):
+        if level == 1:
+            steps += same
+        steps += [(dx, dy) for dx in xs for dy in (level, ny - level)]
+    return (steps if ny > 2 else steps + same) + [(0, 0)]
 
 
 def split_space(size):
@@ -29,7 +39,7 @@
 
 def kernel(
     dims, tok_hbm, gain_ref, w_ref, wout_hbm, scale_ref, cyc_ref, nb_ref, out_ref,
-    tok, wout, packed, place, trade, send, recv, acc, query, keyval, attn, heads,
+    tok, wout, packed, place, trade, send, recv, acc, query, keyval, attn, heads, mixed,
     tok_sem, wout_sem, csem, drem, ssem, rsem, hsem, grem, asem, arem,
 ):
     space, mp, reach = dims
@@ -48,15 +58,15 @@
     third = group // 3
 
     me, head = lax.axis_index("space"), lax.axis_index("mp")
-    core, my_y, my_x = me % 2, (me // 2) % ny, me // (2 * ny)
+    core, my_y, my_x = lax.rem(me, 2), lax.rem(me // 2, ny), me // (2 * ny)
+    steps = chip_steps(nx, ny)
 
     def displaced(j):
-        x = (my_x + far_first(nx, j % nx)) % nx
-        y = (my_y + far_first(ny, j // nx)) % ny
-        return x * ny + y
+        dx, dy = steps[j]
+        return lax.rem(my_x + dx, nx) * ny + lax.rem(my_y + dy, ny)
 
     def ring(t):
-        return (head + far_first(mp, t)) % mp
+        return lax.rem(head + far_static(mp, t), mp)
 
     def token_copy(i):
         part = pl.ds(pl.multiple_of(i * tile, tile), tile)
@@ -74,15 +84,22 @@
             device_id=(displaced(j) * 2 + core, head), device_id_type=MESH,
         )
 
-    def halo(side):
-        if side == 0:
-            src, dst, to = keyval.at[pl.ds(reach, reach)], keyval.at[pl.ds(reach + blocks, reach)], me + space - 1
-        else:
-            src, dst, to = keyval.at[pl.ds(blocks, reach)], keyval.at[pl.ds(0, reach)], me + 1
-        return pltpu.make_async_remote_copy(
-            src_ref=src, dst_ref=dst, send_sem=hsem.at[side], recv_sem=grem.at[side],
-            device_id=(to % space, head), device_id_type=MESH,
-        )
+    def halo(i):
+        per_tile = tile // BLOCK
+        low, high = i * per_tile, (i + 1) * per_tile
+        pieces = []
+        if low < reach:
+            pieces.append((low, min(high, reach) - low, low + reach + blocks, me + space - 1))
+        if high > blocks - reach:
+            first = max(low, blocks - reach)
+            pieces.append((first, high - first, first - (blocks - reach), me + 1))
+        return [
+            pltpu.make_async_remote_copy(
+                src_ref=keyval.at[pl.ds(reach + start, count)], dst_ref=keyval.at[pl.ds(to, count)],
+                send_sem=hsem.at[i, n], recv_sem=grem.at[i, n], device_id=(who % space, head), device_id_type=MESH,
+            )
+            for n, (start, count, to, who) in enumerate(pieces)
+        ]
 
     def output_copy(t):
         return pltpu.make_async_remote_copy(
@@ -91,7 +108,8 @@
         )
 
     def each(start, stop, body):
-        lax.fori_loop(start, stop, lambda i, carry: (body(i), carry)[1], 0)
+        for i in range(start, stop):
+            body(i)
 
     barrier = pltpu.get_barrier_semaphore()
     each(0, chips - 1, lambda j: pl.semaphore_signal(barrier, inc=1, device_id=(displaced(j) * 2 + core, head), device_id_type=MESH))
@@ -104,7 +122,11 @@
     wout_copy.start()
 
     step_ids = lax.broadcasted_iota(jnp.int32, (space, tile), 0)
-    targets = displaced(step_ids // (2 * batch) * batch + step_ids % batch) * 2 + (core + 1 - step_ids // batch % 2) % 2
+    targets = jnp.zeros_like(step_ids)
+    for j in range(chips):
+        start = j // batch * 2 * batch + j % batch
+        chip = displaced(j) * 2
+        targets = jnp.where(step_ids == start, chip + 1 - core, jnp.where(step_ids == start + batch, chip + core, targets))
     before = jnp.where(
         lax.broadcasted_iota(jnp.int32, (tile, tile), 0) < lax.broadcasted_iota(jnp.int32, (tile, tile), 1), 1.0, 0.0
     ).astype(BF16)
@@ -143,7 +165,7 @@
         q = jnp.where(lane == hd, upper, jnp.where(lane == hd + 1, slot - 64 * upper, q))
         packed[part] = jnp.concatenate([kv, q], axis=1).astype(BF16)
 
-    each(0, tiles, project)
+    lax.fori_loop(0, tiles, lambda i, carry: (project(i), carry)[1], 0)
 
     def spread(values):
         return values.reshape(-1, group, BLOCK)
@@ -190,32 +212,35 @@
     lane8 = lax.broadcasted_iota(jnp.int32, (8, BLOCK), 1)
     decode = jnp.where(lane8 == hd, 64.0, jnp.where(lane8 == hd + 1, 1.0, 0.0)).astype(BF16)
     per_tile = tile // BLOCK
-    for g in range(batches):
-        each(g * batch, min((g + 1) * batch, chips - 1), lambda j: exchange(j).wait_recv())
-        got = recv[pl.ds(g * batch, batch)].astype(F32)
-        kv, q = from_message(got.reshape(2 * batch, group + 2 * third, BLOCK))
+    edges = [g * batch for g in range(batches)] + [chips - batch // 2] * (batch > 1) + [chips]
+    centre = [i for n in range((tiles + 1) // 2) for i in dict.fromkeys((n, tiles - 1 - n))]
+    for g, (start, stop) in enumerate(zip(edges, edges[1:])):
+        each(start, min(stop, chips - 1), lambda j: exchange(j).wait_recv())
+        rows = 2 * (stop - start) * group
+        got = recv[start:stop].astype(F32)
+        kv, q = from_message(got.reshape(-1, group + 2 * third, BLOCK))
         kv, q = kv.reshape(rows, BLOCK), q.reshape(rows, BLOCK)
         slot = lax.dot_general(decode, q.astype(BF16), NT, preferred_element_type=F32)[:1]
         got = jnp.concatenate([kv, q], axis=1).astype(BF16)
-        for i in range(tiles):
+        for i in centre:
             part = pl.ds(i * tile, tile)
             index = (lax.broadcasted_iota(jnp.int32, (tile, rows), 0) + i * tile).astype(F32)
             pick = jnp.where(index == slot, 1.0, 0.0).astype(BF16)
             found = jnp.dot(pick, got, preferred_element_type=F32)
             if g > 0:
                 found = acc[part] + found
-            if g < batches - 1:
+            if stop < chips:
                 acc[part] = found
             else:
                 kv = found[:, :BLOCK].astype(BF16)
                 q = jnp.where(lane < hd, found[:, BLOCK:], 0.0).astype(BF16)
                 keyval[pl.ds(reach + i * per_tile, per_tile)] = kv.reshape(per_tile, BLOCK, BLOCK)
                 query[pl.ds(i * per_tile, per_tile)] = q.reshape(per_tile, BLOCK, BLOCK)
-                if (i + 1) * per_tile >= reach > i * per_tile:
-                    halo(0).start()
-    halo(1).start()
-    halo(0).wait_recv()
-    halo(1).wait_recv()
+                for copy in halo(i):
+                    copy.start()
+    for i in range(tiles):
+        for copy in halo(i):
+            copy.wait_recv()
 
     lane_half = lax.broadcasted_iota(jnp.int32, (BLOCK // 2, BLOCK), 1)
 
@@ -223,7 +248,8 @@
         kvs, absent = [], []
         for s in range(neigh):
             nb = nb_ref[b, s]
-            at = (nb - me * blocks + nblk // 2 + nblk) % nblk - nblk // 2 + reach
+            at = nb - me * blocks + reach
+            at = jnp.where(at < 0, at + nblk, jnp.where(at >= blocks + 2 * reach, at - nblk, at))
             kvs.append(keyval[jnp.clip(jnp.where(nb >= 0, at, 0), 0, blocks + 2 * reach - 1)])
             absent.append(jnp.where(nb >= 0, 0.0, -1e30))
         kvs = jnp.concatenate(kvs, axis=0)
@@ -233,38 +259,56 @@
         scores = jnp.concatenate([scores[:, :cut], *tail], axis=1)
         weights = jnp.exp(scores - jnp.max(scores, axis=1, keepdims=True))
         total = jnp.sum(weights, axis=1, keepdims=True)
-        mixed = jnp.dot(weights.astype(BF16), kvs, preferred_element_type=F32) / total
+        values = jnp.dot(weights.astype(BF16), kvs, preferred_element_type=F32) / total
         half = BLOCK // 2
-        return jnp.where(lane_half < hd, pltpu.roll(mixed[:half], hd, 1), mixed[half:]).astype(BF16)
-
-    def attend_send(t):
-        attn[t] = attend(ring(t))
-        output_copy(t).start()
-
-    each(0, mp - 1, attend_send)
-    heads[head] = attend(head)
+        return jnp.where(lane_half < hd, pltpu.roll(values[:half], hd, 1), values[half:]).astype(BF16)
+
+    for t in range(0, mp, 2):
+        blocks_now = [(step, attend(ring(step))) for step in (t, t + 1)]
+        for step, rows_now in blocks_now:
+            if step < mp - 1:
+                attn[step] = rows_now
+                output_copy(step).start()
+            else:
+                heads[head] = rows_now
+
     wout_copy.wait()
-    each(0, mp - 1, lambda t: output_copy(t).wait_recv())
-
-    halves = [], []
-    for h in range(0, mp, 2):
-        low, high = heads[h].astype(F32), heads[h + 1].astype(F32)
-        halves[0].append(jnp.where(lane_half < hd, low, pltpu.roll(high, hd, 1)))
-        halves[1].append(jnp.where(lane_half < hd, pltpu.roll(low, hd, 1), high))
-    rows_in = jnp.concatenate([jnp.concatenate(part, axis=1) for part in halves], axis=0).astype(BF16)
-    out_ref[...] = jnp.dot(rows_in, wout[...], preferred_element_type=F32).astype(BF16)
+    for t in range(0, mp, 2):
+        came = []
+        for step in (t, t + 1):
+            if step < mp - 1:
+                output_copy(step).wait_recv()
+            came.append(lax.rem(head + mp - far_static(mp, step), mp))
+        low, high = (heads[h].astype(F32) for h in came)
+        top = jnp.where(lane_half < hd, low, pltpu.roll(high, hd, 1))
+        bottom = jnp.where(lane_half < hd, pltpu.roll(low, hd, 1), high)
+        pair = jnp.concatenate([top, bottom], axis=0).astype(BF16)
+        weight = jnp.concatenate([wout[pl.ds(pl.multiple_of(h * hd, hd), hd)] for h in came], axis=0)
+        term = jnp.dot(pair, weight, preferred_element_type=F32)
+        if t > 0:
+            term = mixed[...] + term
+        if t < mp - 2:
+            mixed[...] = term
+        else:
+            out_ref[...] = term.astype(BF16)
 
     each(0, batches, lambda g: core_trade(g).wait_send())
     each(0, chips - 1, lambda j: exchange(j).wait_send())
-    halo(0).wait_send()
-    halo(1).wait_send()
+    for i in range(tiles):
+        for copy in halo(i):
+            copy.wait_send()
     each(0, mp - 1, lambda t: output_copy(t).wait_send())
+
+
+def hand_over(mixed_ref, out_ref, sem):
+    copy = pltpu.make_async_copy(mixed_ref, out_ref, sem)
+    copy.start()
+    copy.wait()
 
 
 def per_device(reach, tokens, norm_gain, w_qkv, w_out, head_scale, cycle_to_nested, neighbours):
     space, mp = lax.axis_size("space"), lax.axis_size("mp")
     rows, width = tokens.shape
-    wide = w_out.shape[1]
     group, blocks = rows // space, rows // BLOCK
     tiles = rows // min(256, rows)
     chips = space // 2
@@ -272,9 +316,9 @@
     batches, message = chips // batch, group + 2 * (group // 3)
     vmem, smem, anywhere = (pl.BlockSpec(memory_space=m) for m in (pltpu.VMEM, pltpu.SMEM, pl.ANY))
     dma = pltpu.SemaphoreType.DMA
-    return pl.pallas_call(
+    mixed = pl.pallas_call(
         functools.partial(kernel, (space, mp, reach)),
-        out_shape=jax.ShapeDtypeStruct((rows // mp, wide), BF16),
+        out_shape=jax.ShapeDtypeStruct((rows // mp, w_out.shape[1]), BF16),
         in_specs=[anywhere, vmem, vmem, anywhere, smem, vmem, smem],
         out_specs=vmem,
         scratch_shapes=[
@@ -290,13 +334,17 @@
             pltpu.VMEM((blocks + 2 * reach, BLOCK, BLOCK), BF16),
             pltpu.VMEM((mp, BLOCK // 2, BLOCK), BF16),
             pltpu.VMEM((mp, BLOCK // 2, BLOCK), BF16),
-            dma((tiles,)), dma, dma((batches,)), dma((batches,)), dma((chips,)), dma((chips,)), dma((2,)), dma((2,)), dma((mp,)), dma((mp,)),
+            pltpu.VMEM((rows // mp, w_out.shape[1]), F32),
+            dma((tiles,)), dma, dma((batches,)), dma((batches,)), dma((chips,)), dma((chips,)), dma((tiles, 2)), dma((tiles, 2)), dma((mp,)), dma((mp,)),
         ],
         compiler_params=pltpu.CompilerParams(collective_id=0, has_side_effects=True, vmem_limit_bytes=56 * 2**20),
     )(
         tokens, norm_gain.reshape(1, width), w_qkv.transpose(1, 2, 0).reshape(-1, width), w_out, head_scale,
         cycle_to_nested, neighbours,
     )
+    return pl.pallas_call(
+        hand_over, out_shape=jax.ShapeDtypeStruct(mixed.shape, BF16), in_specs=[anywhere], out_specs=anywhere, scratch_shapes=[dma]
+    )(mixed)
 
 
 def solution(mesh, reach=REACH):

time: 61.4 us -> 67.5 us (1.099)
  Pallas kernels: 58.9 us -> 66.7 us
  local copies, waits for them, and re-layouts: 1.67 us -> 0 us
    pallas_call x0 -> x1, Pallas kernels: none -> 9.05 us  [per_device(): pl.pallas_call(hand_over, out_shape=jax.ShapeDtypeStruct(mixed.shape, BF1...]
    unnamed x1 -> x0, local copies, waits for them, and re-layouts: 1.67 us -> none
    pallas_call x1, Pallas kernels: 58.9 us -> 57.6 us  [per_device(): pl.pallas_call(functools.partial(kernel, (space, mp, reach)), out_shape=j...]
where the time goes in v3:
time: 67.5 us; the launch traced here: 67.3 us
  Pallas kernels  66.7 us (99%)
    pallas_call x1, Pallas kernels, per_device(): pl.pallas_call(functools.partial(kernel, (space, mp, reach)), out_shape=j...  57.6 us
    pallas_call x1, Pallas kernels, per_device(): pl.pallas_call(hand_over, out_shape=jax.ShapeDtypeStruct(mixed.shape, BF1...  9.05 us

profile of v3, /device:TPU:1, one launch (start us, length us, event | category | flops | bytes accessed | tf_op | source)
XLA Modules:
  0.0 67.3 jit_solution(17212998557489274484)
XLA Ops:
  0.7 57.6 %shard_map.73.mixed_ref = bf16[128,1024]{1,0:T(8,128)(2,1)} custom-call(bf16[1536,1024]{1,0:T(8,128)(2,1)} %tok_hbm.1, f32[1,1024]{1,0:T(1,128)} %bitcast.5, bf16[192,1024]{1,0:T(8,128)(2,1)} %bitcast.4, bf16[768,1024]{1,0:T(8,128)(2,1)} %wout_hbm.1, f32[1]{0:T(128)S(6)} %copy.8.scale_ref, s32[1536]{0:T(1024)} %cyc_ref.1, s32[12,9]{1,0:T(8,128)} %nb_ref.1), custom_call_target="tpu_custom_call" | custom-call | tf_op jit(solution)/shard_map/pallas_call | solution.py:319
  58.3 9.1 %shard_map.74 = bf16[128,1024]{1,0:T(8,128)(2,1)} custom-call(bf16[128,1024]{1,0:T(8,128)(2,1)} %shard_map.73.mixed_ref), custom_call_target="tpu_custom_call" | custom-call | tf_op jit(solution)/shard_map/pallas_call | solution.py:345

commit v4 on v3

--- a/solution.py
+++ b/solution.py
@@ -300,12 +300,6 @@
     each(0, mp - 1, lambda t: output_copy(t).wait_send())
 
 
-def hand_over(mixed_ref, out_ref, sem):
-    copy = pltpu.make_async_copy(mixed_ref, out_ref, sem)
-    copy.start()
-    copy.wait()
-
-
 def per_device(reach, tokens, norm_gain, w_qkv, w_out, head_scale, cycle_to_nested, neighbours):
     space, mp = lax.axis_size("space"), lax.axis_size("mp")
     rows, width = tokens.shape
@@ -316,9 +310,9 @@
     batches, message = chips // batch, group + 2 * (group // 3)
     vmem, smem, anywhere = (pl.BlockSpec(memory_space=m) for m in (pltpu.VMEM, pltpu.SMEM, pl.ANY))
     dma = pltpu.SemaphoreType.DMA
-    mixed = pl.pallas_call(
+    return pl.pallas_call(
         functools.partial(kernel, (space, mp, reach)),
-        out_shape=jax.ShapeDtypeStruct((rows // mp, w_out.shape[1]), BF16),
+        out_shape=pltpu.VMEM((rows // mp, w_out.shape[1]), BF16),
         in_specs=[anywhere, vmem, vmem, anywhere, smem, vmem, smem],
         out_specs=vmem,
         scratch_shapes=[
@@ -342,9 +336,6 @@
         tokens, norm_gain.reshape(1, width), w_qkv.transpose(1, 2, 0).reshape(-1, width), w_out, head_scale,
         cycle_to_nested, neighbours,
     )
-    return pl.pallas_call(
-        hand_over, out_shape=jax.ShapeDtypeStruct(mixed.shape, BF16), in_specs=[anywhere], out_specs=anywhere, scratch_shapes=[dma]
-    )(mixed)
 
 
 def solution(mesh, reach=REACH):

time: 67.5 us -> 58.4 us (0.87)
  Pallas kernels: 66.7 us -> 56.9 us
  local copies, waits for them, and re-layouts: 0 us -> 0.71 us
    pallas_call x2 -> x1, Pallas kernels: 66.7 us -> 56.9 us  [per_device(): pl.pallas_call(functools.partial(kernel, (space, mp, reach)), out_shape=p...]
    unnamed x0 -> x1, local copies, waits for them, and re-layouts: none -> 0.71 us
where the time goes in v4:
time: 58.4 us; the launch traced here: 58.2 us
  Pallas kernels  56.9 us (97%)
  local copies, waits for them, and re-layouts  0.71 us (1%)
  between operations  0.66 us (1%)
    pallas_call x1, Pallas kernels, per_device(): pl.pallas_call(functools.partial(kernel, (space, mp, reach)), out_shape=p...  56.9 us

profile of v4, /device:TPU:1, one launch (start us, length us, event | category | flops | bytes accessed | tf_op | source)
XLA Modules:
  0.0 58.2 jit_solution(14145418141614355275)
XLA Ops:
  0.7 56.9 %shard_map.73 = bf16[128,1024]{1,0:T(8,128)(2,1)S(1)} custom-call(bf16[1536,1024]{1,0:T(8,128)(2,1)} %tok_hbm.1, f32[1,1024]{1,0:T(1,128)} %bitcast.5, bf16[192,1024]{1,0:T(8,128)(2,1)} %bitcast.4, bf16[768,1024]{1,0:T(8,128)(2,1)} %wout_hbm.1, f32[1]{0:T(128)S(6)} %copy.10.scale_ref, s32[1536]{0:T(1024)} %cyc_ref.1, s32[12,9]{1,0:T(8,128)} %nb_ref.1), custom_call_target="tpu_custom_call" | custom-call | tf_op jit(solution)/shard_map/pallas_call | solution.py:313
  57.5 0.7 %copy.9 = bf16[128,1024]{1,0:T(8,128)(2,1)} copy(bf16[128,1024]{1,0:T(8,128)(2,1)S(1)} %shard_map.73) | data formatting | bytes 524288

commit v5 on v4

--- a/solution.py
+++ b/solution.py
@@ -273,6 +273,11 @@
                 heads[head] = rows_now
 
     wout_copy.wait()
+    each(0, batches, lambda g: core_trade(g).wait_send())
+    each(0, chips - 1, lambda j: exchange(j).wait_send())
+    for i in range(tiles):
+        for copy in halo(i):
+            copy.wait_send()
     for t in range(0, mp, 2):
         came = []
         for step in (t, t + 1):
@@ -292,11 +297,6 @@
         else:
             out_ref[...] = term.astype(BF16)
 
-    each(0, batches, lambda g: core_trade(g).wait_send())
-    each(0, chips - 1, lambda j: exchange(j).wait_send())
-    for i in range(tiles):
-        for copy in halo(i):
-            copy.wait_send()
     each(0, mp - 1, lambda t: output_copy(t).wait_send())
 
 

time: 58.4 us -> 58.3 us (level)
  no operation moved by 1% of the time
where the time goes in v5:
time: 58.3 us; the launch traced here: 58.2 us
  Pallas kernels  56.8 us (97%)
  local copies, waits for them, and re-layouts  0.71 us (1%)
  between operations  0.66 us (1%)
    pallas_call x1, Pallas kernels, per_device(): pl.pallas_call(functools.partial(kernel, (space, mp, reach)), out_shape=p...  56.8 us

profile of v5, /device:TPU:1, one launch (start us, length us, event | category | flops | bytes accessed | tf_op | source)
XLA Modules:
  0.0 58.2 jit_solution(758282795519971247)
XLA Ops:
  0.7 56.8 %shard_map.73 = bf16[128,1024]{1,0:T(8,128)(2,1)S(1)} custom-call(bf16[1536,1024]{1,0:T(8,128)(2,1)} %tok_hbm.1, f32[1,1024]{1,0:T(1,128)} %bitcast.5, bf16[192,1024]{1,0:T(8,128)(2,1)} %bitcast.4, bf16[768,1024]{1,0:T(8,128)(2,1)} %wout_hbm.1, f32[1]{0:T(128)S(6)} %copy.10.scale_ref, s32[1536]{0:T(1024)} %cyc_ref.1, s32[12,9]{1,0:T(8,128)} %nb_ref.1), custom_call_target="tpu_custom_call" | custom-call | tf_op jit(solution)/shard_map/pallas_call | solution.py:313
  57.5 0.7 %copy.9 = bf16[128,1024]{1,0:T(8,128)(2,1)} copy(bf16[128,1024]{1,0:T(8,128)(2,1)S(1)} %shard_map.73) | data formatting | bytes 524288
